TPU v7x, 256 devices: a whole 4x4x8 slice. The times are simulated.
256 devices in a mesh: row: 16 (over x, z_hi, core), col: 16 (over z_lo, y).
Axes of the slice: x: 4, y: 4, z: 8 (z_hi: 2, z_lo: 4; z = z_hi * 4 + z_lo), core: 2. Of those that a mesh axis runs over, the one named last changes fastest.
Arguments:
- latent: bfloat16 [256, 256, 512], P('row', 'col'), may hold values from -6 to 6
- grad_latent: bfloat16 [256, 256, 512], P('row', 'col'), may hold values from -6 to 6
- w_qkv_row: bfloat16 [512, 1536], replicated, may hold values from -0.25 to 0.25
- w_out_row: bfloat16 [512, 512], replicated, may hold values from -0.25 to 0.25
- w_qkv_col: bfloat16 [512, 1536], replicated, may hold values from -0.25 to 0.25
- w_out_col: bfloat16 [512, 512], replicated, may hold values from -0.25 to 0.25
Outputs:
- final: bfloat16 [256, 256, 512], P('row', 'col')
- grad_input: bfloat16 [256, 256, 512], P('row', 'col')
- grad_qkv_row: float32 [512, 1536], P('row', 'col')
- grad_out_row: float32 [512, 512], P('row', 'col')
- grad_qkv_col: float32 [512, 1536], P('row', 'col')
- grad_out_col: float32 [512, 512], P('row', 'col')
All inputs are finite; a program needn't handle non-finite values.
Results may differ from a plain program's by a relative error of at most 0.04.
Values may be sent and summed in bfloat16 or wider, within the bound.
No kernel may reach another device: no remote copies, remote signals or barrier semaphores. Data moves between devices by JAX's collectives and lax.ppermute only.
A program may use at most 128 MiB of HBM per device.

v0:
```python
import math

import jax
import jax.numpy as jnp
from jax import lax
from jax.sharding import PartitionSpec as P

HEADS = 8
HD = 64


EPS = 1e-06


def rms_rows(values):
    return values * lax.rsqrt(jnp.mean(values * values, axis=-1, keepdims=True) + EPS)


def head_norm(qkv):
    parts = qkv.reshape(qkv.shape[:-1] + (3, HEADS, HD))
    scale = lax.rsqrt(jnp.mean(parts * parts, axis=-1, keepdims=True) + EPS)
    keep = (jnp.arange(3) == 2)[:, None, None]
    normed = jnp.where(keep, parts, parts * scale)
    return normed.reshape(qkv.shape)


def attention(qkvn, form):
    lead = qkvn.shape[:-1]
    parts = qkvn.astype(jnp.float32).reshape(lead + (3, HEADS, HD))
    query = parts[..., 0, :, :]
    keys = parts[..., 1, :, :]
    values = parts[..., 2, :, :]
    if form == "row":
        scores = jnp.einsum("bqhe,bkhe->bhqk", query, keys) / math.sqrt(HD)
    else:
        scores = jnp.einsum("qbhe,kbhe->bhqk", query, keys) / math.sqrt(HD)
    expo = jnp.exp(scores)
    weights = expo / jnp.sum(expo, axis=-1, keepdims=True)
    rounded = lax.optimization_barrier(weights.astype(jnp.bfloat16)).astype(jnp.float32)
    if form == "row":
        mixed = jnp.einsum("bhqk,bkhe->bqhe", rounded, values)
    else:
        mixed = jnp.einsum("bhqk,kbhe->qbhe", rounded, values)
    return mixed.reshape(lead + (HEADS * HD,))


def to_rows(values):
    return lax.all_to_all(values, "col", split_axis=0, concat_axis=1, tiled=True)


def from_rows(values):
    return lax.all_to_all(values, "col", split_axis=1, concat_axis=0, tiled=True)


def to_cols(values):
    return lax.all_to_all(values, "row", split_axis=1, concat_axis=0, tiled=True)


def from_cols(values):
    return lax.all_to_all(values, "row", split_axis=0, concat_axis=1, tiled=True)


def reduce_grads(grads):
    partial_sums = (
        lax.psum_scatter(
            grads[0].astype(jnp.bfloat16), "col", scatter_dimension=1, tiled=True
        ).astype(jnp.float32),
        lax.psum_scatter(
            grads[1].astype(jnp.bfloat16), "col", scatter_dimension=1, tiled=True
        ).astype(jnp.float32),
        lax.psum_scatter(
            grads[2].astype(jnp.bfloat16), "col", scatter_dimension=1, tiled=True
        ).astype(jnp.float32),
        lax.psum_scatter(
            grads[3].astype(jnp.bfloat16), "col", scatter_dimension=1, tiled=True
        ).astype(jnp.float32),
    )
    return (
        lax.psum_scatter(
            partial_sums[0].astype(jnp.bfloat16), "row", scatter_dimension=0, tiled=True
        ).astype(jnp.float32),
        lax.psum_scatter(
            partial_sums[1].astype(jnp.bfloat16), "row", scatter_dimension=0, tiled=True
        ).astype(jnp.float32),
        lax.psum_scatter(
            partial_sums[2].astype(jnp.bfloat16), "row", scatter_dimension=0, tiled=True
        ).astype(jnp.float32),
        lax.psum_scatter(
            partial_sums[3].astype(jnp.bfloat16), "row", scatter_dimension=0, tiled=True
        ).astype(jnp.float32),
    )


def sublayer_forward(latent_in, w_qkv, w_out, there, back, form):
    normed = rms_rows(latent_in.astype(jnp.float32)).astype(jnp.bfloat16)
    qkv = jnp.dot(normed, w_qkv, preferred_element_type=jnp.float32)
    qkvn = there(head_norm(qkv).astype(jnp.bfloat16))
    mixed = back(attention(qkvn, form).astype(jnp.bfloat16))
    result = latent_in.astype(jnp.float32) + jnp.dot(
        mixed, w_out, preferred_element_type=jnp.float32
    )
    return (result.astype(jnp.bfloat16), (normed, qkv, qkvn, mixed))


def sublayer_backward(latent_in, grad_out, w_qkv, w_out, saved, there, back, form):
    used, qkv, qkvn, mixed = saved
    grad_w_out = jnp.einsum("abd,abe->de", mixed, grad_out, preferred_element_type=jnp.float32)
    grad_mixed = jnp.einsum(
        "abe,de->abd", grad_out, w_out, preferred_element_type=jnp.float32
    ).astype(jnp.bfloat16)
    moved_grad = there(grad_mixed)
    _, pull = jax.vjp(lambda a: attention(a, form), qkvn)
    grad_qkvn = pull(moved_grad.astype(jnp.float32))[0]
    home_grad = back(grad_qkvn)
    _, pull_norm = jax.vjp(head_norm, qkv)
    grad_qkv = pull_norm(home_grad.astype(jnp.float32))[0].astype(jnp.bfloat16)
    grad_w_qkv = jnp.einsum("abd,abe->de", used, grad_qkv, preferred_element_type=jnp.float32)
    grad_normed = jnp.einsum(
        "abe,de->abd", grad_qkv, w_qkv, preferred_element_type=jnp.float32
    ).astype(jnp.bfloat16)
    _, pull_rms = jax.vjp(rms_rows, latent_in.astype(jnp.float32))
    grad_x = grad_out.astype(jnp.float32) + pull_rms(grad_normed.astype(jnp.float32))[0]
    return (grad_x.astype(jnp.bfloat16), grad_w_qkv, grad_w_out)


def on_device(latent, grad_latent, w_qkv_row, w_out_row, w_qkv_col, w_out_col):
    middle, saved_row = sublayer_forward(latent, w_qkv_row, w_out_row, to_rows, from_rows, "row")
    final, saved_col = sublayer_forward(middle, w_qkv_col, w_out_col, to_cols, from_cols, "col")
    grad_middle, grad_qkv_col, grad_out_col = sublayer_backward(
        middle, grad_latent, w_qkv_col, w_out_col, saved_col, to_cols, from_cols, "col"
    )
    grad_input, grad_qkv_row, grad_out_row = sublayer_backward(
        latent, grad_middle, w_qkv_row, w_out_row, saved_row, to_rows, from_rows, "row"
    )
    grad_qkv_row, grad_out_row, grad_qkv_col, grad_out_col = reduce_grads(
        (grad_qkv_row, grad_out_row, grad_qkv_col, grad_out_col)
    )
    return (final, grad_input, grad_qkv_row, grad_out_row, grad_qkv_col, grad_out_col)


def solution(mesh):
    in_specs = (P("row", "col", None), P("row", "col", None), P(), P(), P(), P())
    out_specs = (
        P("row", "col", None),
        P("row", "col", None),
        P("row", "col"),
        P("row", "col"),
        P("row", "col"),
        P("row", "col"),
    )
    return jax.shard_map(
        on_device, mesh=mesh, in_specs=in_specs, out_specs=out_specs, check_vma=False
    )
```

profile of v0, /device:TPU:8, one launch (start us, length us, event | category | flops | bytes accessed | tf_op | source)
XLA Modules:
  0.0 872.3 jit_solution(6838819424681235694)
XLA Ops:
  27.8 28.8 %all_to_all.96 = bf16[16,16,1536]{2,1,0:T(8,128)(2,1)} all-to-all(bf16[16,16,1536]{2,1,0:T(8,128)(2,1)S(1)} %fusion.14), channel_id=1, replica_groups=mesh['row'=16,'col'=16] {'col'}, dimensions={0} | all-to-all | bytes 1572864 | tf_op jit(solution)/shard_map/all_to_all | solution.py:48
  72.8 5.9 all-to-all-start.1
  81.0 6.3 all-to-all-done.1
  88.0 8.6 all-to-all-start.4
  121.7 9.8 %all-to-all-start.2 = ((bf16[16,16,1536]{2,0,1:T(8,128)(2,1)}), bf16[16,16,1536]{2,0,1:T(8,128)(2,1)}, u32[]{:S(2)}, u32[]{:S(2)}) async-start(bf16[16,16,1536]{2,0,1:T(8,128)(2,1)} %copy.174), calls=%async_computation.2 | async-start | bytes 1572864 | tf_op jit(solution)/shard_map/all_to_all | solution.py:56
  135.6 16.7 %all-to-all-done.2 = bf16[16,16,1536]{2,0,1:T(8,128)(2,1)} async-done(((bf16[16,16,1536]{2,0,1:T(8,128)(2,1)}), bf16[16,16,1536]{2,0,1:T(8,128)(2,1)}, u32[]{:S(2)}, u32[]{:S(2)}) %all-to-all-start.2) | async-done | bytes 786464 | tf_op jit(solution)/shard_map/all_to_all | solution.py:56
  180.6 4.9 all-to-all-start.3
  200.5 9.8 %all-to-all-start.5 = ((bf16[16,2,12288]{2,1,0:T(2,128)(2,1)}), bf16[16,2,12288]{2,1,0:T(2,128)(2,1)}, u32[]{:S(2)}, u32[]{:S(2)}) async-start(bf16[16,2,12288]{2,1,0:T(2,128)(2,1)} %reshape.382), calls=%async_computation.5 | async-start | bytes 1572864 | tf_op jit(solution)/shard_map/all_to_all | solution.py:60
  217.1 10.8 %all-to-all-done.5 = bf16[16,2,12288]{2,1,0:T(2,128)(2,1)} async-done(((bf16[16,2,12288]{2,1,0:T(2,128)(2,1)}), bf16[16,2,12288]{2,1,0:T(2,128)(2,1)}, u32[]{:S(2)}, u32[]{:S(2)}) %all-to-all-start.5) | async-done | bytes 786464 | tf_op jit(solution)/shard_map/all_to_all | solution.py:60
  228.0 5.2 reshape.383
  241.1 4.8 multiply_reduce_fusion.1
  265.4 14.8 %all-to-all-start.6 = ((bf16[16,16,512]{2,1,0:T(8,128)(2,1)}), bf16[16,16,512]{2,1,0:T(8,128)(2,1)S(1)}, u32[]{:S(2)}, u32[]{:S(2)}) async-start(bf16[16,16,512]{2,1,0:T(8,128)(2,1)} %convolution_convert_fusion.2), calls=%async_computation.6 | async-start | bytes 524288 | tf_op jit(solution)/shard_map/all_to_all | solution.py:48
  280.7 21.3 %reduce-scatter.23.cloned.1.call-done = bf16[512,32]{0,1:T(8,128)(2,1)} async-done(((bf16[512,512]{0,1:T(8,128)(2,1)}), bf16[512,32]{0,1:T(8,128)(2,1)}) %reduce-scatter.23.cloned.1.call-update) | async-done | bytes 32784 | tf_op jit(solution)/shard_map/reduce_scatter | solution.py:74
  314.2 6.3 reduce.11
  323.8 8.8 %all-to-all-start.7 = ((bf16[16,2,12288]{2,1,0:T(2,128)(2,1)}), bf16[16,2,12288]{2,1,0:T(2,128)(2,1)}, u32[]{:S(2)}, u32[]{:S(2)}) async-start(bf16[16,2,12288]{2,1,0:T(2,128)(2,1)} %reshape.384), calls=%async_computation.7 | async-start | bytes 1572864 | tf_op jit(solution)/shard_map/all_to_all | solution.py:52
  332.7 53.0 %reduce-scatter.19.cloned.1.call-done = bf16[512,32]{0,1:T(8,128)(2,1)} async-done(((bf16[512,512]{0,1:T(8,128)(2,1)}), bf16[512,32]{0,1:T(8,128)(2,1)}) %reduce-scatter.19.cloned.1.call-update) | async-done | bytes 32784 | tf_op jit(solution)/shard_map/reduce_scatter | solution.py:68
  389.4 5.2 reshape.385
  394.6 7.1 convert_reduce_fusion
  425.5 40.0 %reduce-scatter.31.cloned.1.call-done = bf16[32,32]{1,0:T(8,128)(2,1)} async-done(((bf16[512,32]{1,0:T(8,128)(2,1)}), bf16[32,32]{1,0:T(8,128)(2,1)}) %reduce-scatter.31.cloned.1.call-update) | async-done | bytes 2064
  466.9 74.6 %reduce-scatter.27.cloned.1.call-done = bf16[32,32]{1,0:T(8,128)(2,1)} async-done(((bf16[512,32]{1,0:T(8,128)(2,1)}), bf16[32,32]{1,0:T(8,128)(2,1)}) %reduce-scatter.27.cloned.1.call-update) | async-done | bytes 2064
  545.1 77.3 %reduce-scatter.21.cloned.1.call-done = bf16[512,96]{0,1:T(8,128)(2,1)} async-done(((bf16[512,1536]{0,1:T(8,128)(2,1)}), bf16[512,96]{0,1:T(8,128)(2,1)}) %reduce-scatter.21.cloned.1.call-update) | async-done | bytes 98320 | tf_op jit(solution)/shard_map/reduce_scatter | solution.py:71
  624.1 83.6 %reduce-scatter.17.cloned.1.call-done = bf16[512,96]{0,1:T(8,128)(2,1)} async-done(((bf16[512,1536]{0,1:T(8,128)(2,1)}), bf16[512,96]{0,1:T(8,128)(2,1)}) %reduce-scatter.17.cloned.1.call-update) | async-done | bytes 98320 | tf_op jit(solution)/shard_map/reduce_scatter | solution.py:65
  710.3 77.3 %reduce-scatter.29.cloned.1.call-done = bf16[32,96]{1,0:T(8,128)(2,1)} async-done(((bf16[512,96]{1,0:T(8,128)(2,1)}), bf16[32,96]{1,0:T(8,128)(2,1)}) %reduce-scatter.29.cloned.1.call-update) | async-done | bytes 6160
  789.1 74.7 %reduce-scatter.25.cloned.1.call-done = bf16[32,96]{1,0:T(8,128)(2,1)} async-done(((bf16[512,96]{1,0:T(8,128)(2,1)}), bf16[32,96]{1,0:T(8,128)(2,1)}) %reduce-scatter.25.cloned.1.call-update) | async-done | bytes 6160
  (225 shorter events, 201.5 us)
Async XLA Ops:
  7.2 92.8 %copy-start = (bf16[512,1536]{1,0:T(8,128)(2,1)S(1)}, bf16[512,1536]{1,0:T(8,128)(2,1)}, u32[]{:S(2)}) copy-start(bf16[512,1536]{1,0:T(8,128)(2,1)} %param.10) | copy-start | bytes 4718596
  10.9 15.2 %copy-start.1 = (f32[16,16,1536]{2,1,0:T(8,128)}, f32[16,16,1536]{2,1,0:T(8,128)S(1)}, u32[]{:S(2)}) copy-start(f32[16,16,1536]{2,1,0:T(8,128)S(1)} %fusion.26) | copy-start | bytes 4718596
  72.8 26.0 %copy-start.14 = (bf16[16,16,512]{2,1,0:T(8,128)(2,1)S(1)}, bf16[16,16,512]{2,1,0:T(8,128)(2,1)}, u32[]{:S(2)}) copy-start(bf16[16,16,512]{2,1,0:T(8,128)(2,1)} %param.6) | copy-start | bytes 786436
  72.8 14.5 %all-to-all-start.1 = ((bf16[16,2,4096]{2,1,0:T(2,128)(2,1)}), bf16[16,2,4096]{2,1,0:T(2,128)(2,1)S(1)}, u32[]{:S(2)}, u32[]{:S(2)}) async-start(bf16[16,2,4096]{2,1,0:T(2,128)(2,1)} %reshape.380), calls=%async_computation.1 | async-start | bytes 524288 | tf_op jit(solution)/shard_map/all_to_all | solution.py:52
  78.7 20.2 %copy-start.29 = (bf16[512,512]{1,0:T(8,128)(2,1)S(1)}, bf16[512,512]{1,0:T(8,128)(2,1)}, u32[]{:S(2)}) copy-start(bf16[512,512]{1,0:T(8,128)(2,1)} %param.9) | copy-start | bytes 1572868
  88.0 33.8 %all-to-all-start.4 = ((bf16[16,16,512]{2,0,1:T(8,128)(2,1)}), bf16[16,16,512]{2,0,1:T(8,128)(2,1)}, u32[]{:S(2)}, u32[]{:S(2)}) async-start(bf16[16,16,512]{2,0,1:T(8,128)(2,1)} %copy.181), calls=%async_computation.4 | async-start | bytes 524288 | tf_op jit(solution)/shard_map/all_to_all | solution.py:56
  121.7 30.6 %all-to-all-start.2 = ((bf16[16,16,1536]{2,0,1:T(8,128)(2,1)}), bf16[16,16,1536]{2,0,1:T(8,128)(2,1)}, u32[]{:S(2)}, u32[]{:S(2)}) async-start(bf16[16,16,1536]{2,0,1:T(8,128)(2,1)} %copy.174), calls=%async_computation.2 | async-start | bytes 1572864 | tf_op jit(solution)/shard_map/all_to_all | solution.py:56
  180.6 19.9 %all-to-all-start.3 = ((bf16[16,2,4096]{2,1,0:T(2,128)(2,1)}), bf16[16,2,4096]{2,1,0:T(2,128)(2,1)}, u32[]{:S(2)}, u32[]{:S(2)}) async-start(bf16[16,2,4096]{2,1,0:T(2,128)(2,1)} %reshape.386), calls=%async_computation.3 | async-start | bytes 524288 | tf_op jit(solution)/shard_map/all_to_all | solution.py:60
  200.5 27.5 %all-to-all-start.5 = ((bf16[16,2,12288]{2,1,0:T(2,128)(2,1)}), bf16[16,2,12288]{2,1,0:T(2,128)(2,1)}, u32[]{:S(2)}, u32[]{:S(2)}) async-start(bf16[16,2,12288]{2,1,0:T(2,128)(2,1)} %reshape.382), calls=%async_computation.5 | async-start | bytes 1572864 | tf_op jit(solution)/shard_map/all_to_all | solution.py:60
  210.2 91.8 %reduce-scatter.23.cloned.1.call-start = ((), (), s32[]{:S(2)}) async-start(), calls=%async_computation.19 | async-start | bytes 557056 | tf_op jit(solution)/shard_map/reduce_scatter | solution.py:74
  217.1 168.6 %reduce-scatter.19.cloned.1.call-start = ((), (), s32[]{:S(2)}) async-start(), calls=%async_computation.17 | async-start | bytes 557056 | tf_op jit(solution)/shard_map/reduce_scatter | solution.py:68
  263.2 40.7 %copy-start.18 = (bf16[16,16,512]{2,1,0:T(8,128)(2,1)}, bf16[16,16,512]{2,1,0:T(8,128)(2,1)S(1)}, u32[]{:S(2)}) copy-start(bf16[16,16,512]{2,1,0:T(8,128)(2,1)S(1)} %fusion.54) | copy-start | bytes 786436
  264.3 39.9 %copy-start.24 = (bf16[1,256,1,8,64]{1,4,3,2,0:T(8,128)(2,1)S(1)}, bf16[1,256,1,8,64]{1,4,3,2,0:T(8,128)(2,1)}, u32[]{:S(2)}) copy-start(bf16[1,256,1,8,64]{1,4,3,2,0:T(8,128)(2,1)} %copy-done.23) | copy-start | bytes 786436
  265.4 38.2 %all-to-all-start.6 = ((bf16[16,16,512]{2,1,0:T(8,128)(2,1)}), bf16[16,16,512]{2,1,0:T(8,128)(2,1)S(1)}, u32[]{:S(2)}, u32[]{:S(2)}) async-start(bf16[16,16,512]{2,1,0:T(8,128)(2,1)} %convolution_convert_fusion.2), calls=%async_computation.6 | async-start | bytes 524288 | tf_op jit(solution)/shard_map/all_to_all | solution.py:48
  280.2 185.2 %reduce-scatter.31.cloned.1.call-start = ((), (), s32[]{:S(2)}) async-start(), calls=%async_computation.23 | async-start | bytes 139264
  320.5 66.8 %copy-start.9 = (f32[16,16,512]{2,1,0:T(8,128)S(1)}, f32[16,16,512]{2,1,0:T(8,128)}, u32[]{:S(2)}) copy-start(f32[16,16,512]{2,1,0:T(8,128)} %copy-done.7) | copy-start | bytes 1572868
  320.5 66.8 %copy-start.16 = (bf16[16,16,1536]{2,1,0:T(8,128)(2,1)S(1)}, bf16[16,16,1536]{2,1,0:T(8,128)(2,1)}, u32[]{:S(2)}) copy-start(bf16[16,16,1536]{2,1,0:T(8,128)(2,1)} %copy-done.15) | copy-start | bytes 2359300
  323.8 65.5 %all-to-all-start.7 = ((bf16[16,2,12288]{2,1,0:T(2,128)(2,1)}), bf16[16,2,12288]{2,1,0:T(2,128)(2,1)}, u32[]{:S(2)}, u32[]{:S(2)}) async-start(bf16[16,2,12288]{2,1,0:T(2,128)(2,1)} %reshape.384), calls=%async_computation.7 | async-start | bytes 1572864 | tf_op jit(solution)/shard_map/all_to_all | solution.py:52
  332.7 208.8 %reduce-scatter.27.cloned.1.call-start = ((), (), s32[]{:S(2)}) async-start(), calls=%async_computation.21 | async-start | bytes 139264
  387.2 235.1 %reduce-scatter.21.cloned.1.call-start = ((), (), s32[]{:S(2)}) async-start(), calls=%async_computation.18 | async-start | bytes 1671168 | tf_op jit(solution)/shard_map/reduce_scatter | solution.py:71
  389.1 318.5 %reduce-scatter.17.cloned.1.call-start = ((), (), s32[]{:S(2)}) async-start(), calls=%async_computation.16 | async-start | bytes 1671168 | tf_op jit(solution)/shard_map/reduce_scatter | solution.py:65
  423.3 364.3 %reduce-scatter.29.cloned.1.call-start = ((), (), s32[]{:S(2)}) async-start(), calls=%async_computation.22 | async-start | bytes 139264
  425.5 283.9 %copy-start.19 = (bf16[16,16,512]{2,1,0:T(8,128)(2,1)S(1)}, bf16[16,16,512]{2,1,0:T(8,128)(2,1)}, u32[]{:S(2)}) copy-start(bf16[16,16,512]{2,1,0:T(8,128)(2,1)} %copy-done.18) | copy-start | bytes 786436
  624.0 239.8 %reduce-scatter.25.cloned.1.call-start = ((), (), s32[]{:S(2)}) async-start(), calls=%async_computation.20 | async-start | bytes 139264
  (32 other events, 86.8 us)
Sparse Core Ops, SparseCore 0:
  217.2 84.7 reduce-scatter.22
  304.7 80.9 reduce-scatter.18
  389.7 75.7 reduce-scatter.30
  469.8 71.6 reduce-scatter.26
  543.9 78.3 reduce-scatter.20
  624.9 82.7 reduce-scatter.16
  711.7 75.8 reduce-scatter.28
  792.1 71.5 reduce-scatter.24
where the time goes:
time: 883 us; the launch traced here: 872 us
  waiting for transfers between devices  536 us (61%)
  local copies, waits for them, and re-layouts  135 us (15%)
  other arithmetic  63.7 us (7%)
  starting transfers between devices  63.5 us (7%)
  matrix products  30.1 us (3%)
  blocking collectives  28.8 us (3%)
  between operations  15 us (2%)
    unnamed x12, waiting for transfers between devices  267 us
    reduce_scatter x1, waiting for transfers between devices, reduce_grads(): lax.psum_scatter(grads[0].astype(jnp.bfloat16), 'col', scatter_dimension=...  83.6 us
    reduce_scatter x1, waiting for transfers between devices, reduce_grads(): lax.psum_scatter(grads[2].astype(jnp.bfloat16), 'col', scatter_dimension=...  77.3 us
    unnamed x114, local copies, waits for them, and re-layouts  62.9 us
    reduce_scatter x1, waiting for transfers between devices, reduce_grads(): lax.psum_scatter(grads[1].astype(jnp.bfloat16), 'col', scatter_dimension=...  53 us
    all_to_all x1, blocking collectives, to_rows(): lax.all_to_all(values, 'col', split_axis=0, concat_axis=1, tiled=True)  28.8 us
    reduce_scatter x1, waiting for transfers between devices, reduce_grads(): lax.psum_scatter(grads[3].astype(jnp.bfloat16), 'col', scatter_dimension=...  21.3 us
    all_to_all x2, starting transfers between devices, to_cols(): lax.all_to_all(values, 'row', split_axis=1, concat_axis=0, tiled=True)  18.3 us
  transfers between devices with their start and end apart: 15, of which 11 were waited for; matrix products, arithmetic and copies ran while one was open for 18% of the time, Pallas kernels for 0%

commit v1 on v0

v1 whole, which is shorter than its diff:
```python
import functools

import jax
import jax.numpy as jnp
from jax import lax
from jax.experimental import pallas as pl
from jax.experimental.pallas import tpu as pltpu
from jax.sharding import Mesh
from jax.sharding import PartitionSpec as P

HEADS = 8
HD = 64
CH = 512
EPS = 1e-06
F32 = jnp.float32
BF16 = jnp.bfloat16

ROW = ("x", "zh", "core")
COL = ("zl", "y")
CHIP = ("zl", "y", "x", "zh")


def nn(a, b):
    return jnp.dot(a, b, preferred_element_type=F32)


def nt(a, b):
    return lax.dot_general(a, b, (((1,), (1,)), ((), ())), preferred_element_type=F32)


def tn(a, b):
    return lax.dot_general(a, b, (((0,), (0,)), ((), ())), preferred_element_type=F32)


def split2(a):
    hi = a.astype(BF16)
    return hi, (a - hi.astype(F32)).astype(BF16)


def iota(shape, dim):
    return lax.broadcasted_iota(jnp.int32, shape, dim)


def head_map():
    shape = (2 * CH, 128)
    return (iota(shape, 0) // HD == iota(shape, 1)).astype(BF16)


def head_mean(values, heads):
    hi, lo = split2(values)
    return (nn(hi, heads) + nn(lo, heads)) * (1.0 / HD)


def head_spread(values, heads):
    hi, lo = split2(values)
    return nt(hi, heads) + nt(lo, heads)


def inv_rms(x):
    return lax.rsqrt(jnp.mean(x * x, axis=-1, keepdims=True) + EPS)


def swap_order(values):
    rows = iota((256, 256), 0)
    cols = iota((256, 256), 1)
    swap = ((rows & 15) * 16 + (rows >> 4) == cols).astype(BF16)
    return nn(swap, values).astype(BF16)


def project(x, w_qkv, heads):
    normed = (x * inv_rms(x)).astype(BF16)
    qkv = nn(normed, w_qkv)
    qk = qkv[:, : 2 * CH]
    scale = lax.rsqrt(head_mean(qk * qk, heads) + EPS)
    qkn = (qk * head_spread(scale, heads)).astype(BF16)
    return normed, scale, qkn, qkv[:, 2 * CH :].astype(BF16)


def low_half():
    return iota((256, 128), 1) < HD


def only(half, values):
    low = low_half()
    keep = low if half == 0 else jnp.logical_not(low)
    return jnp.where(keep, values, jnp.zeros_like(values))


def softmax(query, keys):
    expo = jnp.exp(nt(query, keys) * 0.125)
    return expo * (1.0 / jnp.sum(expo, axis=-1, keepdims=True))


def attend(qkn, v, pair):
    at = slice(pair * 128, pair * 128 + 128)
    q2, k2, v2 = qkn[:, at], qkn[:, CH + pair * 128 : CH + pair * 128 + 128], v[:, at]
    parts = [nn(softmax(only(h, q2), k2).astype(BF16), v2) for h in range(2)]
    return jnp.where(low_half(), parts[0], parts[1])


def attend_back(qkn, v, gmix, gmix_t, q_t, pair, mixed=None):
    at = slice(pair * 128, pair * 128 + 128)
    q2, k2, v2 = qkn[:, at], qkn[:, CH + pair * 128 : CH + pair * 128 + 128], v[:, at]
    g2 = gmix[:, at]
    g2f = g2.astype(F32)
    low = low_half()
    mix, gq, gk, gv = [], [], [], []
    for h in range(2):
        rows = slice(pair * 128 + h * HD, pair * 128 + h * HD + HD)
        weights = softmax(only(h, q2), k2)
        rounded = weights.astype(BF16)
        mix.append(nn(rounded, v2))
        gweights = nt(only(h, g2), v2)
        inner = jnp.sum(only(h, g2f * mix[h]), axis=-1, keepdims=True)
        gscores = (weights * (gweights - inner) * 0.125).astype(BF16)
        gv.append(nn(gmix_t[rows], rounded))
        gq.append(nn(gscores, k2))
        gk.append(nn(q_t[rows], gscores))
    return (
        jnp.where(low, mix[0], mix[1]),
        jnp.where(low, gq[0], gq[1]),
        jnp.concatenate(gk, axis=0),
        jnp.concatenate(gv, axis=0),
    )


def forward_kernel(x_ref, wq_ref, wo_ref, mid_ref, normed_ref, scale_ref, qkn_ref, v_ref, mixed_ref):
    x = x_ref[...].astype(F32)
    heads = head_map()
    normed, scale, qkn, v = project(x, wq_ref[...], heads)
    normed_ref[...] = normed
    scale_ref[...] = scale
    qkn_ref[...] = qkn
    v_ref[...] = v
    for pair in range(HEADS // 2):
        mixed_ref[:, pair * 128 : pair * 128 + 128] = attend(qkn, v, pair).astype(BF16)
    y = (x + nn(mixed_ref[...], wo_ref[...])).astype(BF16)
    mid_ref[...] = swap_order(y)


def backward_tail(x, g, wq_ref, scale, qkn, v, gmix, gmix_t, heads, mixed_ref, gqkv_ref, gx_ref):
    q_t = qkn[:, :CH].T
    gqs, gks, gvs = [], [], []
    for pair in range(HEADS // 2):
        mix, gq, gk, gv = attend_back(qkn, v, gmix, gmix_t, q_t, pair)
        if mixed_ref is not None:
            mixed_ref[:, pair * 128 : pair * 128 + 128] = mix.astype(BF16)
        gqs.append(gq.astype(BF16))
        gks.append(gk.astype(BF16).T)
        gvs.append(gv.astype(BF16).T)
    gqk = jnp.concatenate(gqs + gks, axis=1).astype(F32)
    yn = qkn.astype(F32)
    inner = head_spread(head_mean(yn * gqk, heads), heads)
    gqk = head_spread(scale, heads) * (gqk - yn * inner)
    gqkv_ref[:, : 2 * CH] = gqk.astype(BF16)
    gqkv_ref[:, 2 * CH :] = jnp.concatenate(gvs, axis=1)
    gnormed = nt(gqkv_ref[...], wq_ref[...]).astype(BF16).astype(F32)
    r = inv_rms(x)
    xn = x * r
    gx = g + r * (gnormed - xn * jnp.mean(xn * gnormed, axis=-1, keepdims=True))
    gx_ref[...] = gx.astype(BF16)


def both_kernel(x_ref, g_ref, wq_ref, wo_ref, y_ref, gx_ref, normed_ref, mixed_ref, gqkv_ref):
    x = x_ref[...].astype(F32)
    heads = head_map()
    normed, scale, qkn, v = project(x, wq_ref[...], heads)
    normed_ref[...] = normed
    g = g_ref[...]
    gmix = nt(g, wo_ref[...]).astype(BF16)
    gmix_t = nt(wo_ref[...], g).astype(BF16)
    backward_tail(
        x, g.astype(F32), wq_ref, scale, qkn, v, gmix, gmix_t, heads, mixed_ref, gqkv_ref, gx_ref
    )
    y_ref[...] = (x + nn(mixed_ref[...], wo_ref[...])).astype(BF16)


def back_kernel(x_ref, g_ref, wq_ref, wo_ref, scale_ref, qkn_ref, v_ref, gx_ref, gqkv_ref, gs_ref):
    g = swap_order(g_ref[...])
    gs_ref[...] = g
    gmix = nt(g, wo_ref[...]).astype(BF16)
    gmix_t = nt(wo_ref[...], g).astype(BF16)
    backward_tail(
        x_ref[...].astype(F32),
        g.astype(F32),
        wq_ref,
        scale_ref[...],
        qkn_ref[...],
        v_ref[...],
        gmix,
        gmix_t,
        head_map(),
        None,
        gqkv_ref,
        gx_ref,
    )


def weights_kernel(place, core_ref, normed_ref, mixed_ref, gqkv_ref, g_ref, keep_ref, send_ref):
    core = core_ref[0]
    row = iota((CH, CH), 0)
    col = iota((CH, CH), 1)
    bit = (col >> 8) ^ core
    order = (row == ((col >> 5) & 7) * 64 + bit * 32 + (col & 31)).astype(BF16)
    normed = nn(normed_ref[...], order).astype(BF16)
    mixed = nn(mixed_ref[...], order).astype(BF16)
    col3 = iota((384, CH), 1)
    lane3 = col3 & 127
    spread3 = ((iota((384, CH), 0) == (col3 >> 7) * 96 + lane3) & (lane3 < 96)).astype(BF16)
    col1 = iota((128, CH), 1)
    lane1 = col1 & 127
    spread1 = ((iota((128, CH), 0) == (col1 >> 7) * 32 + lane1 - 96) & (lane1 >= 96)).astype(BF16)
    for group in range(4):
        gq = nn(gqkv_ref[:, group * 384 : group * 384 + 384], spread3).astype(BF16)
        gg = nn(g_ref[:, group * 128 : group * 128 + 128], spread1).astype(BF16)
        total = (tn(normed, gq) + tn(mixed, gg)).astype(BF16)
        for slot, ref in ((0, keep_ref), (1, send_ref)):
            for xz in range(8):
                rows = slice(slot * 256 + xz * 32, slot * 256 + xz * 32 + 32)
                for y in range(4):
                    ref[place(group, y, xz >> 1, xz & 1)] = total[rows, y * 128 : y * 128 + 128]


VMEM = pl.BlockSpec(memory_space=pltpu.VMEM)
SMEM = pl.BlockSpec(memory_space=pltpu.SMEM)


def shape(rows, cols, dtype=BF16):
    return jax.ShapeDtypeStruct((rows, cols), dtype)


def call(kernel, outs, specs, flops, args):
    nbytes = sum(a.size * a.dtype.itemsize for a in (*args, *outs))
    return pl.pallas_call(
        kernel,
        out_shape=outs,
        in_specs=specs,
        out_specs=[VMEM] * len(outs),
        compiler_params=pltpu.CompilerParams(vmem_limit_bytes=48 * 2**20),
        cost_estimate=pl.CostEstimate(flops=flops, bytes_accessed=nbytes, transcendentals=2**19),
    )(*args)


def weight_terms(place, core, normed, mixed, gqkv, g):
    outs = [jax.ShapeDtypeStruct((128, 32, 128), BF16)] * 2
    return call(
        functools.partial(weights_kernel, place),
        outs,
        [SMEM] + [VMEM] * 4,
        2 * 10**9,
        (core, normed, mixed, gqkv, g),
    )


def swap_cores(values):
    return lax.ppermute(values, "core", [(0, 1), (1, 0)])


def a2a(values, axes):
    return lax.all_to_all(values, axes, split_axis=0, concat_axis=0, tiled=True)


def add(a, b):
    return (a.astype(F32) + b.astype(F32)).astype(BF16)


def chip_place(zl, y, x, zh):
    return ((zl * 4 + y) * 4 + x) * 2 + zh


def ring_place(zl, y, x, zh):
    return ((y * 4 + x) * 2 + zh) * 4 + zl


def on_device(latent, grad_latent, w_qkv_row, w_out_row, w_qkv_col, w_out_col):
    core = lax.axis_index("core").astype(jnp.int32).reshape(1)
    x_row = a2a(latent, COL).reshape(256, CH)
    g_col = a2a(jnp.swapaxes(grad_latent, 0, 1), ROW).reshape(256, CH)
    mid_row, normed_r, scale_r, qkn_r, v_r, mixed_r = call(
        forward_kernel,
        [
            shape(256, CH),
            shape(256, CH),
            shape(256, 128, F32),
            shape(256, 2 * CH),
            shape(256, CH),
            shape(256, CH),
        ],
        [VMEM] * 3,
        10**9,
        (x_row, w_qkv_row, w_out_row),
    )
    x_col = a2a(mid_row, ROW + COL)
    y_col, gx_col, normed_c, mixed_c, gqkv_c = call(
        both_kernel,
        [shape(256, CH)] * 4 + [shape(256, 3 * CH)],
        [VMEM] * 4,
        3 * 10**9,
        (x_col, g_col, w_qkv_col, w_out_col),
    )
    g_row = a2a(gx_col, ROW + COL)
    keep_c, send_c = weight_terms(ring_place, core, normed_c, mixed_c, gqkv_c, g_col)
    sum_c = add(keep_c, swap_cores(send_c)).reshape(4, 4, 8, 32, 128)
    sum_c = lax.psum_scatter(sum_c, "y", scatter_dimension=0, tiled=False)
    sum_c = lax.psum_scatter(sum_c, "x", scatter_dimension=0, tiled=False)
    sum_c = lax.psum_scatter(sum_c, ("zh", "zl"), scatter_dimension=0, tiled=False).astype(F32)
    final = jnp.swapaxes(a2a(y_col.reshape(16, 16, CH), ROW), 0, 1)
    gx_row, gqkv_r, gs_r = call(
        back_kernel,
        [shape(256, CH), shape(256, 3 * CH), shape(256, CH)],
        [VMEM] * 7,
        2 * 10**9,
        (x_row, g_row, w_qkv_row, w_out_row, scale_r, qkn_r, v_r),
    )
    grad_input = a2a(gx_row.reshape(16, 16, CH), COL)
    keep_r, send_r = weight_terms(chip_place, core, normed_r, mixed_r, gqkv_r, gs_r)
    sum_r = a2a(add(keep_r, swap_cores(send_r)), CHIP)
    sum_r = jnp.sum(sum_r.astype(F32), axis=0)
    return (final, grad_input, sum_r[:, :96], sum_r[:, 96:], sum_c[:, :96], sum_c[:, 96:])


def solution(mesh):
    fine = Mesh(mesh.devices.reshape(4, 2, 2, 4, 4), ("x", "zh", "core", "zl", "y"))
    in_specs = (P(ROW, COL, None), P(ROW, COL, None), P(), P(), P(), P())
    out_specs = (
        P(ROW, COL, None),
        P(ROW, COL, None),
        P(ROW, COL),
        P(ROW, COL),
        P(ROW, COL),
        P(ROW, COL),
    )
    return jax.shard_map(
        on_device, mesh=fine, in_specs=in_specs, out_specs=out_specs, check_vma=False
    )
```

time: 883 us -> 243 us (0.28); the launches traced: 872 us -> 241 us
  waiting for transfers between devices: 536 us -> 114 us
  local copies, waits for them, and re-layouts: 135 us -> 20.9 us
  other arithmetic: 63.7 us -> 7.57 us
  matrix products: 30.1 us -> 0 us
  Pallas kernels: 0 us -> 23.9 us
  starting transfers between devices: 63.5 us -> 43.2 us
  blocking collectives: 28.8 us -> 18.3 us
    unnamed x12 -> x3, waiting for transfers between devices: 267 us -> 0.7 us
    reduce_scatter x4 -> x3, waiting for transfers between devices: 235 us -> 62.8 us  [the longest x1 36.6 us: on_device(): lax.psum_scatter(sum_c, ('zh', 'zl'), scatter_dimension=0, tiled=False)]
    unnamed x114 -> x55, local copies, waits for them, and re-layouts: 62.9 us -> 19 us
    dot_general x24 -> x0, matrix products: 30.1 us -> none  [the longest x3 6.23 us: attention(): mixed = jnp.einsum('bhqk,kbhe->qbhe', rounded, values)]
    pallas_call x0 -> x5, Pallas kernels: none -> 23.9 us  [call(): pl.pallas_call(kernel, out_shape=outs, in_specs=specs, out_specs=[VMEM] *...]
    convert_element_type x14 -> x3, other arithmetic: 27.5 us -> 5.66 us  [the longest x2 4.96 us: add(): return (a.astype(F32) + b.astype(F32)).astype(BF16)]
    reduce_sum x7 -> x1, other arithmetic: 21.9 us -> 0.19 us  [on_device(): sum_r = jnp.sum(sum_r.astype(F32), axis=0)]
    all_to_all x7 -> x6, starting transfers between devices: 62.5 us -> 42.6 us  [a2a(): return lax.all_to_all(values, axes, split_axis=0, concat_axis=0, tiled=True)]
  transfers between devices with their start and end apart: 15 -> 11, of which waited for: 11 -> 8; matrix products, arithmetic and copies ran while one was open for 18% -> 6% of each run, Pallas kernels for 0% -> 6%
where the time goes in v1:
time: 243 us; the launch traced here: 241 us
  waiting for transfers between devices  114 us (47%)
  starting transfers between devices  43.2 us (18%)
  Pallas kernels  23.9 us (10%)
  local copies, waits for them, and re-layouts  20.9 us (9%)
  blocking collectives  18.3 us (8%)
  between operations  13.9 us (6%)
  other arithmetic  7.57 us (3%)
    all_to_all x6, waiting for transfers between devices, a2a(): return lax.all_to_all(values, axes, split_axis=0, concat_axis=0, tiled=True)  50 us
    all_to_all x6, starting transfers between devices, a2a(): return lax.all_to_all(values, axes, split_axis=0, concat_axis=0, tiled=True)  42.6 us
    reduce_scatter x1, waiting for transfers between devices, on_device(): lax.psum_scatter(sum_c, ('zh', 'zl'), scatter_dimension=0, tiled=False)  36.6 us
    reduce_scatter x1, waiting for transfers between devices, on_device(): sum_c = lax.psum_scatter(sum_c, 'x', scatter_dimension=0, tiled=False)  26.2 us
    pallas_call x5, Pallas kernels, call(): pl.pallas_call(kernel, out_shape=outs, in_specs=specs, out_specs=[VMEM] *...  23.9 us
    unnamed x55, local copies, waits for them, and re-layouts  19 us
    all_to_all x1, blocking collectives, a2a(): return lax.all_to_all(values, axes, split_axis=0, concat_axis=0, tiled=True)  18.3 us
    convert_element_type x2, other arithmetic, add(): return (a.astype(F32) + b.astype(F32)).astype(BF16)  4.96 us
  transfers between devices with their start and end apart: 11, of which 8 were waited for; matrix products, arithmetic and copies ran while one was open for 6% of the time, Pallas kernels for 6%

profile of v1, /device:TPU:8, one launch (start us, length us, event | category | flops | bytes accessed | tf_op | source)
XLA Modules:
  0.0 241.4 jit_solution(17633162163865659993)
XLA Ops:
  7.2 18.3 %all_to_all.47 = bf16[16,16,512]{2,1,0:T(8,128)(2,1)S(1)} all-to-all(bf16[16,16,512]{2,1,0:T(8,128)(2,1)} %param.6), channel_id=1, replica_groups=mesh['x'=4,'zh'=2,'core'=2,'zl'=4,'y'=4] {'zl','y'}, dimensions={0} | all-to-all | bytes 524288 | tf_op jit(solution)/shard_map/all_to_all | solution.py:260
  25.5 1.4 copy-done.1
  27.9 2.6 %shard_map.109 = (bf16[256,512]{1,0:T(8,128)(2,1)S(1)}, bf16[256,512]{1,0:T(8,128)(2,1)S(1)}, f32[256,128]{1,0:T(8,128)S(1)}, bf16[256,1024]{1,0:T(8,128)(2,1)S(...) custom-call(bf16[256,512]{1,0:T(8,128)(2,1)S(1)} %bitcast.29, bf16[512,1536]{1,0:T(8,128)(2,1)S(1)} %copy-done.1, ...), custom_call_target="tpu_custom_call" | custom-call | flops 1000000000 | bytes 4063232 | tf_op jit(solution)/shard_map/pallas_call | solution.py:234
  34.8 11.0 %all-to-all-start.1 = ((bf16[256,2,256]{2,1,0:T(2,128)(2,1)}), bf16[256,2,256]{2,1,0:T(2,128)(2,1)S(1)}, u32[]{:S(2)}, u32[]{:S(2)}) async-start(bf16[256,2,256]{2,1,0:T(2,128)(2,1)} %reshape.43), calls=%async_computation.1 | async-start | bytes 524288 | tf_op jit(solution)/shard_map/all_to_all | solution.py:260
  46.7 14.1 %all-to-all-done.1 = bf16[256,2,256]{2,1,0:T(2,128)(2,1)S(1)} async-done(((bf16[256,2,256]{2,1,0:T(2,128)(2,1)}), bf16[256,2,256]{2,1,0:T(2,128)(2,1)S(1)}, u32[]{:S(2)}, u32[]{:S(2)}) %all-to-all-start.1) | async-done | bytes 262176 | tf_op jit(solution)/shard_map/all_to_all | solution.py:260
  60.8 3.5 %all-to-all-start.2 = ((bf16[16,16,512]{2,1,0:T(8,128)(2,1)}), bf16[16,16,512]{2,1,0:T(8,128)(2,1)S(1)}, u32[]{:S(2)}, u32[]{:S(2)}) async-start(bf16[16,16,512]{2,1,0:T(8,128)(2,1)} %bitcast.22), calls=%async_computation.2 | async-start | bytes 524288 | tf_op jit(solution)/shard_map/all_to_all | solution.py:260
  66.4 10.0 %all-to-all-done.2 = bf16[16,16,512]{2,1,0:T(8,128)(2,1)S(1)} async-done(((bf16[16,16,512]{2,1,0:T(8,128)(2,1)}), bf16[16,16,512]{2,1,0:T(8,128)(2,1)S(1)}, u32[]{:S(2)}, u32[]{:S(2)}) %all-to-all-start.2) | async-done | bytes 262176 | tf_op jit(solution)/shard_map/all_to_all | solution.py:260
  76.4 7.6 %shard_map.110 = (bf16[256,512]{1,0:T(8,128)(2,1)}, bf16[256,512]{1,0:T(8,128)(2,1)S(1)}, bf16[256,512]{1,0:T(8,128)(2,1)S(1)}, bf16[256,512]{1,0:T(8,128)(2,1)S(1)}, bf16[256,1536]{1,0:T(8,128)(2,1)S(1)}) custom-call(bf16[256,512]{1,0:T(8,128)(2,1)S(1)} %bitcast.25, bf16[256,512]{1,0:T(8,128)(2,1)S(1)} %bitcast.31, bf16[512,1536]{1,0:T(8,128)(2,1)S(1)} %copy-done, ...), custom_call_target="tpu_custom_call" | custom-call | flops 3000000000 | bytes 4456448 | tf_op jit(solution)/shard_map/pallas_call | solution.py:234
  87.3 9.4 %all-to-all-start.4 = ((bf16[256,2,256]{2,1,0:T(2,128)(2,1)}), bf16[256,2,256]{2,1,0:T(2,128)(2,1)}, u32[]{:S(2)}, u32[]{:S(2)}) async-start(bf16[256,2,256]{2,1,0:T(2,128)(2,1)} %reshape.45), calls=%async_computation.4 | async-start | bytes 524288 | tf_op jit(solution)/shard_map/all_to_all | solution.py:260
  97.8 4.0 %shard_map.113 = (bf16[128,32,128]{2,1,0:T(8,128)(2,1)S(1)}, bf16[128,32,128]{2,1,0:T(8,128)(2,1)}) custom-call(s32[1]{0:T(128)} %bitcast.8.core_ref, bf16[256,512]{1,0:T(8,128)(2,1)S(1)} %copy-done.17, bf16[256,512]{1,0:T(8,128)(2,1)S(1)} %copy-done.19, bf16[256,1536]{1,0:T(8,128)(2,1)S(1)} %copy-done.15, bf16[256,512]{1,0:T(8,128)(2,1)S(1)} %bitcast.32), custom_call_target="tpu_custom_call" | custom-call | flops 2000000000 | bytes 3670020 | tf_op jit(solution)/shard_map/pallas_call | solution.py:234
  101.9 9.0 %all-to-all-done.4 = bf16[256,2,256]{2,1,0:T(2,128)(2,1)} async-done(((bf16[256,2,256]{2,1,0:T(2,128)(2,1)}), bf16[256,2,256]{2,1,0:T(2,128)(2,1)}, u32[]{:S(2)}, u32[]{:S(2)}) %all-to-all-start.4) | async-done | bytes 262176 | tf_op jit(solution)/shard_map/all_to_all | solution.py:260
  110.9 2.8 %reshape.46 = bf16[256,1,512]{2,1,0:T(2,128)(2,1)} reshape(bf16[256,2,256]{2,1,0:T(2,128)(2,1)} %all-to-all-done.4) | data formatting | bytes 524288
  116.7 6.8 %shard_map.111 = (bf16[256,512]{1,0:T(8,128)(2,1)}, bf16[256,1536]{1,0:T(8,128)(2,1)S(1)}, bf16[256,512]{1,0:T(8,128)(2,1)S(1)}) custom-call(bf16[256,512]{1,0:T(8,128)(2,1)S(1)} %bitcast.30, bf16[256,512]{1,0:T(8,128)(2,1)S(1)} %bitcast.26, bf16[512,1536]{1,0:T(8,128)(2,1)S(1)} %copy-done.2, bf16[512,512]{1,0:T(8,128)(2,1)S(1)} %copy-done.5, ...), custom_call_target="tpu_custom_call" | custom-call | flops 2000000000 | bytes 4849664 | tf_op jit(solution)/shard_map/pallas_call | solution.py:234
  123.6 3.0 %shard_map.112 = (bf16[128,32,128]{2,1,0:T(8,128)(2,1)S(1)}, bf16[128,32,128]{2,1,0:T(8,128)(2,1)S(1)}) custom-call(s32[1]{0:T(128)} %bitcast.8.core_ref, bf16[256,512]{1,0:T(8,128)(2,1)S(1)} %copy-done.9, bf16[256,512]{1,0:T(8,128)(2,1)S(1)} %copy-done.11, bf16[256,1536]{1,0:T(8,128)(2,1)S(1)} %get-tuple-element.33.gqkv_ref, ...), custom_call_target="tpu_custom_call" | custom-call | flops 2000000000 | bytes 3670020 | tf_op jit(solution)/shard_map/pallas_call | solution.py:234
  126.7 3.5 %all-to-all-start.3 = ((bf16[16,16,512]{2,1,0:T(8,128)(2,1)}), bf16[16,16,512]{2,1,0:T(8,128)(2,1)S(1)}, u32[]{:S(2)}, u32[]{:S(2)}) async-start(bf16[16,16,512]{2,1,0:T(8,128)(2,1)} %bitcast.4), calls=%async_computation.3 | async-start | bytes 524288 | tf_op jit(solution)/shard_map/all_to_all | solution.py:260
  130.5 2.5 %add_convert_fusion = bf16[128,32,128]{2,1,0:T(8,128)(2,1)} fusion(bf16[128,32,128]{2,1,0:T(8,128)(2,1)} %collective-permute-done.1, bf16[128,32,128]{2,1,0:T(8,128)(2,1)S(1)} %get-tuple-element.40), kind=kLoop, calls=%fused_computation | loop fusion | flops 2097152 | bytes 3145728 | tf_op jit(solution)/shard_map/convert_element_type | solution.py:264
  133.0 9.3 %all-to-all-done.3 = bf16[16,16,512]{2,1,0:T(8,128)(2,1)S(1)} async-done(((bf16[16,16,512]{2,1,0:T(8,128)(2,1)}), bf16[16,16,512]{2,1,0:T(8,128)(2,1)S(1)}, u32[]{:S(2)}, u32[]{:S(2)}) %all-to-all-start.3) | async-done | bytes 262176 | tf_op jit(solution)/shard_map/all_to_all | solution.py:260
  142.3 7.6 %all-to-all-start.5 = ((bf16[16,16,512]{2,1,0:T(8,128)(2,1)}), bf16[16,16,512]{2,1,0:T(8,128)(2,1)S(1)}, u32[]{:S(2)}, u32[]{:S(2)}) async-start(bf16[16,16,512]{2,1,0:T(8,128)(2,1)} %bitcast.7), calls=%async_computation.5 | async-start | bytes 524288 | tf_op jit(solution)/shard_map/all_to_all | solution.py:260
  149.9 2.5 %add_convert_fusion.1 = bf16[128,32,128]{2,1,0:T(8,128)(2,1)} fusion(bf16[128,32,128]{2,1,0:T(8,128)(2,1)} %collective-permute-done, bf16[128,32,128]{2,1,0:T(8,128)(2,1)S(1)} %get-tuple-element.35), kind=kLoop, calls=%fused_computation.2 | loop fusion | flops 2097152 | bytes 3145728 | tf_op jit(solution)/shard_map/convert_element_type | solution.py:264
  152.4 6.5 %all-to-all-done.5 = bf16[16,16,512]{2,1,0:T(8,128)(2,1)S(1)} async-done(((bf16[16,16,512]{2,1,0:T(8,128)(2,1)}), bf16[16,16,512]{2,1,0:T(8,128)(2,1)S(1)}, u32[]{:S(2)}, u32[]{:S(2)}) %all-to-all-start.5) | async-done | bytes 262176 | tf_op jit(solution)/shard_map/all_to_all | solution.py:260
  158.8 7.5 %all-to-all-start.6 = ((bf16[128,32,128]{2,1,0:T(8,128)(2,1)}), bf16[128,32,128]{2,1,0:T(8,128)(2,1)S(1)}, u32[]{:S(2)}, u32[]{:S(2)}) async-start(bf16[128,32,128]{2,1,0:T(8,128)(2,1)} %add_convert_fusion.1), calls=%async_computation.6 | async-start | bytes 2097152 | tf_op jit(solution)/shard_map/all_to_all | solution.py:260
  168.0 26.2 %reduce-scatter.6.cloned.1.call-done = bf16[1,8,32,128]{3,2,1,0:T(8,128)(2,1)} async-done(((bf16[4,8,32,128]{3,2,1,0:T(8,128)(2,1)}), bf16[1,8,32,128]{3,2,1,0:T(8,128)(2,1)}) %reduce-scatter.6.cloned.1.call-update) | async-done | bytes 65552 | tf_op jit(solution)/shard_map/reduce_scatter | solution.py:305
  194.2 1.1 all-to-all-done.6
  196.2 36.6 %reduce-scatter.8.cloned.1.call-done = bf16[1,32,128]{2,1,0:T(8,128)(2,1)} async-done(((bf16[8,32,128]{2,1,0:T(8,128)(2,1)}), bf16[1,32,128]{2,1,0:T(8,128)(2,1)}) %reduce-scatter.8.cloned.1.call-update) | async-done | bytes 8208 | tf_op jit(solution)/shard_map/reduce_scatter | solution.py:306
  (71 shorter events, 20.6 us)
Async XLA Ops:
  25.5 1.4 copy-start.1
  32.7 13.2 %copy-start.20 = (bf16[16,16,512]{2,1,0:T(8,128)(2,1)S(1)}, bf16[16,16,512]{2,1,0:T(8,128)(2,1)}, u32[]{:S(2)}) copy-start(bf16[16,16,512]{2,1,0:T(8,128)(2,1)} %param.7) | copy-start | bytes 786436
  34.8 41.6 %copy-start = (bf16[512,1536]{1,0:T(8,128)(2,1)S(1)}, bf16[512,1536]{1,0:T(8,128)(2,1)}, u32[]{:S(2)}) copy-start(bf16[512,1536]{1,0:T(8,128)(2,1)} %wq_ref.4) | copy-start | bytes 4718596
  34.8 41.6 %copy-start.3 = (bf16[512,512]{1,0:T(8,128)(2,1)S(1)}, bf16[512,512]{1,0:T(8,128)(2,1)}, u32[]{:S(2)}) copy-start(bf16[512,512]{1,0:T(8,128)(2,1)} %wo_ref.4) | copy-start | bytes 1572868
  34.8 26.0 %all-to-all-start.1 = ((bf16[256,2,256]{2,1,0:T(2,128)(2,1)}), bf16[256,2,256]{2,1,0:T(2,128)(2,1)S(1)}, u32[]{:S(2)}, u32[]{:S(2)}) async-start(bf16[256,2,256]{2,1,0:T(2,128)(2,1)} %reshape.43), calls=%async_computation.1 | async-start | bytes 524288 | tf_op jit(solution)/shard_map/all_to_all | solution.py:260
  60.8 15.6 %all-to-all-start.2 = ((bf16[16,16,512]{2,1,0:T(8,128)(2,1)}), bf16[16,16,512]{2,1,0:T(8,128)(2,1)S(1)}, u32[]{:S(2)}, u32[]{:S(2)}) async-start(bf16[16,16,512]{2,1,0:T(8,128)(2,1)} %bitcast.22), calls=%async_computation.2 | async-start | bytes 524288 | tf_op jit(solution)/shard_map/all_to_all | solution.py:260
  85.6 11.2 %copy-start.16 = (bf16[256,512]{1,0:T(8,128)(2,1)}, bf16[256,512]{1,0:T(8,128)(2,1)S(1)}, u32[]{:S(2)}) copy-start(bf16[256,512]{1,0:T(8,128)(2,1)S(1)} %get-tuple-element.37.normed_ref) | copy-start | bytes 786436
  85.6 11.2 %copy-start.15 = (bf16[256,1536]{1,0:T(8,128)(2,1)S(1)}, bf16[256,1536]{1,0:T(8,128)(2,1)}, u32[]{:S(2)}) copy-start(bf16[256,1536]{1,0:T(8,128)(2,1)} %copy-done.14) | copy-start | bytes 2359300
  85.6 11.2 %copy-start.19 = (bf16[256,512]{1,0:T(8,128)(2,1)S(1)}, bf16[256,512]{1,0:T(8,128)(2,1)}, u32[]{:S(2)}) copy-start(bf16[256,512]{1,0:T(8,128)(2,1)} %copy-done.18) | copy-start | bytes 786436
  87.3 23.5 %all-to-all-start.4 = ((bf16[256,2,256]{2,1,0:T(2,128)(2,1)}), bf16[256,2,256]{2,1,0:T(2,128)(2,1)}, u32[]{:S(2)}, u32[]{:S(2)}) async-start(bf16[256,2,256]{2,1,0:T(2,128)(2,1)} %reshape.45), calls=%async_computation.4 | async-start | bytes 524288 | tf_op jit(solution)/shard_map/all_to_all | solution.py:260
  97.8 16.9 %copy-start.5 = (bf16[512,512]{1,0:T(8,128)(2,1)S(1)}, bf16[512,512]{1,0:T(8,128)(2,1)}, u32[]{:S(2)}) copy-start(bf16[512,512]{1,0:T(8,128)(2,1)} %wo_ref.5) | copy-start | bytes 1572868
  101.7 13.0 %copy-start.2 = (bf16[512,1536]{1,0:T(8,128)(2,1)S(1)}, bf16[512,1536]{1,0:T(8,128)(2,1)}, u32[]{:S(2)}) copy-start(bf16[512,1536]{1,0:T(8,128)(2,1)} %wq_ref.5) | copy-start | bytes 4718596
  101.7 28.7 %collective-permute-start.1 = (bf16[128,32,128]{2,1,0:T(8,128)(2,1)}, bf16[128,32,128]{2,1,0:T(8,128)(2,1)}, u32[]{:S(2)}, u32[]{:S(2)}) collective-permute-start(bf16[128,32,128]{2,1,0:T(8,128)(2,1)} %get-tuple-element.41), channel_id=1, source_target_pairs={{0,16},{16,0},{1,17},{17,1},{2,18},{18,2},{3,19},{19,3},{4,20},{20... | collective-permute-start | bytes 3145736 | tf_op jit(solution)/shard_map/ppermute | solution.py:256
  116.7 6.8 %copy-start.9 = (bf16[256,512]{1,0:T(8,128)(2,1)S(1)}, bf16[256,512]{1,0:T(8,128)(2,1)}, u32[]{:S(2)}) copy-start(bf16[256,512]{1,0:T(8,128)(2,1)} %copy-done.8) | copy-start | bytes 786436
  116.7 6.9 %copy-start.11 = (bf16[256,512]{1,0:T(8,128)(2,1)S(1)}, bf16[256,512]{1,0:T(8,128)(2,1)}, u32[]{:S(2)}) copy-start(bf16[256,512]{1,0:T(8,128)(2,1)} %copy-done.10) | copy-start | bytes 786436
  126.5 23.3 %collective-permute-start = (bf16[128,32,128]{2,1,0:T(8,128)(2,1)S(1)}, bf16[128,32,128]{2,1,0:T(8,128)(2,1)}, u32[]{:S(2)}, u32[]{:S(2)}) collective-permute-start(bf16[128,32,128]{2,1,0:T(8,128)(2,1)S(1)} %get-tuple-element.36), channel_id=1, source_target_pairs={{0,16},{16,0},{1,17},{17,1},{2,18},{18,2},{3,19},{19,3},{4,20},{20... | collective-permute-start | bytes 3145736 | tf_op jit(solution)/shard_map/ppermute | solution.py:256
  126.7 15.7 %all-to-all-start.3 = ((bf16[16,16,512]{2,1,0:T(8,128)(2,1)}), bf16[16,16,512]{2,1,0:T(8,128)(2,1)S(1)}, u32[]{:S(2)}, u32[]{:S(2)}) async-start(bf16[16,16,512]{2,1,0:T(8,128)(2,1)} %bitcast.4), calls=%async_computation.3 | async-start | bytes 524288 | tf_op jit(solution)/shard_map/all_to_all | solution.py:260
  130.2 36.2 %reduce-scatter.4.cloned.1.call-start = ((), (), s32[]{:S(2)}) async-start(), calls=%async_computation.10 | async-start | bytes 1310720 | tf_op jit(solution)/shard_map/reduce_scatter | solution.py:304
  142.3 16.5 %all-to-all-start.5 = ((bf16[16,16,512]{2,1,0:T(8,128)(2,1)}), bf16[16,16,512]{2,1,0:T(8,128)(2,1)S(1)}, u32[]{:S(2)}, u32[]{:S(2)}) async-start(bf16[16,16,512]{2,1,0:T(8,128)(2,1)} %bitcast.7), calls=%async_computation.5 | async-start | bytes 524288 | tf_op jit(solution)/shard_map/all_to_all | solution.py:260
  158.8 36.5 %all-to-all-start.6 = ((bf16[128,32,128]{2,1,0:T(8,128)(2,1)}), bf16[128,32,128]{2,1,0:T(8,128)(2,1)S(1)}, u32[]{:S(2)}, u32[]{:S(2)}) async-start(bf16[128,32,128]{2,1,0:T(8,128)(2,1)} %add_convert_fusion.1), calls=%async_computation.6 | async-start | bytes 2097152 | tf_op jit(solution)/shard_map/all_to_all | solution.py:260
  166.4 27.8 %reduce-scatter.6.cloned.1.call-start = ((), (), s32[]{:S(2)}) async-start(), calls=%async_computation.11 | async-start | bytes 327680 | tf_op jit(solution)/shard_map/reduce_scatter | solution.py:305
  167.1 65.7 %reduce-scatter.8.cloned.1.call-start = ((), (), s32[]{:S(2)}) async-start(), calls=%async_computation.12 | async-start | bytes 73728 | tf_op jit(solution)/shard_map/reduce_scatter | solution.py:306
  195.5 39.4 %copy-start.21 = (f32[32,128]{1,0:T(8,128)}, f32[32,128]{1,0:T(8,128)S(1)}, u32[]{:S(2)}) copy-start(f32[32,128]{1,0:T(8,128)S(1)} %convert_reduce_fusion) | copy-start | bytes 49156
  233.5 1.4 copy-start.22
  (10 other events, 9.1 us)
Sparse Core Ops, SparseCore 0:
  133.6 26.0 reduce-scatter.3
  169.9 24.2 reduce-scatter.5
  196.7 36.1 reduce-scatter.7
